TPU v7x, 32 devices: a whole 2x2x4 slice. The times are simulated.
32 devices in a mesh: station: 32 (over z, y, x, core), sample: 1.
Axes of the slice: x: 2, y: 2, z: 4, core: 2. Of those that a mesh axis runs over, the one named last changes fastest.
Arguments:
- flux: bfloat16 [4, 1024, 3584], P('sample', 'station'), may hold values from -6 to 6
- coeff: float32 [1024, 3584], P('station'), may hold values from 0.02 to 0.24
- diff_steps: int32 [4], P('sample'), may hold values from 3 to 6, as said below
- footprint: bfloat16 [512, 4, 16384], P('station'), may hold values from -0.03125 to 0.03125
- tile_src: int32 [512, 4, 1], replicated, may hold values from 0 to 31; in each aligned block of 64 rows (0 to 63, 64 to 127, ..., all dimensions but the last counted through in order) at most 4 rows name the same one
- tile_local: int32 [512, 4], replicated, may hold values from 0 to 6
- tile_count: int32 [512], P('station'), may hold values from 1 to 4
Outputs:
- observed: float32 [512, 4], P('station')
Inputs may be any that keep to these rules, and one draw needn't show every extreme that they name: `tile_src`: in each aligned block of 64 rows (the slots of one index's stations, stations and slots in order), no band appears more than 4 times, and some band appears exactly 4 times. `diff_steps`: some sample takes 6 steps and another takes 3.
All inputs are finite; a program needn't handle non-finite values.
Results may differ from a plain program's by a relative error of at most 0.0029.
Values may be sent and summed in bfloat16 or wider, within the bound.
A program may use at most 128 MiB of HBM per device.

v0:
```python
import jax
import jax.numpy as jnp
from jax import lax
from jax.sharding import PartitionSpec as P

TILE_LON = 512
TILES_DEV = 7
KT = 4
ITERS = 6


def extended_2(cells, sides, width):
    for axis, dim in sides:
        count = lax.axis_size(axis)
        ends = count - 1
        head = lax.slice_in_dim(cells, 0, width, axis=dim)
        tail = lax.slice_in_dim(cells, cells.shape[dim] - width, cells.shape[dim], axis=dim)
        cells = jnp.concatenate(
            [
                lax.ppermute(tail, axis, [(i, (i + 1) % count) for i in range(ends)]),
                cells,
                lax.ppermute(head, axis, [((i + 1) % count, i) for i in range(ends)]),
            ],
            axis=dim,
        )
    return cells


def diffuse_rows(extended, gates):
    field = extended[:-1]
    coefs = extended[-1]
    center = field[:, 1:-1]
    lap = (
        field[:, :-2]
        + field[:, 2:]
        + jnp.roll(center, 1, 2)
        + jnp.roll(center, -1, 2)
        - 4.0 * center
    )
    update = gates[:, None, None] * coefs[None, 1:-1] * lap
    return (center + update, coefs[1:-1])


def body(flux, coeff, diff_steps, footprint, tile_src, tile_local, tile_count):
    samples_here, rows_here, lon_count = flux.shape
    stations_here = footprint.shape[0]
    devices = lax.axis_size("station")
    own_index = lax.axis_index("station")
    cap_slots = 2 * max(1, (stations_here * KT + devices - 1) // devices)
    field = flux.astype(jnp.float32)
    for step_index in range(ITERS):
        gates = (step_index < diff_steps).astype(jnp.float32)
        stacked = jnp.concatenate([field, coeff[None]], axis=0)
        extended = extended_2(stacked, (("station", 1),), 1)
        field, unused = diffuse_rows(extended, gates)
    final = field.astype(jnp.bfloat16)
    tiles = final.reshape(samples_here, rows_here, TILES_DEV, TILE_LON)
    tiles = tiles.transpose(2, 0, 1, 3).reshape(TILES_DEV, samples_here, rows_here * TILE_LON)
    slot_count = stations_here * KT
    order = jnp.arange(slot_count, dtype=jnp.int32)
    src_all = tile_src[:, :, 0].reshape(devices, slot_count)
    loc_all = tile_local.reshape(devices, slot_count)
    earlier = order[None, :] < order[:, None]
    same_src = src_all[:, :, None] == src_all[:, None, :]
    rank_all = jnp.sum((same_src & earlier[None]).astype(jnp.int32), axis=2)
    cap_range = jnp.arange(cap_slots, dtype=jnp.int32)
    band_range = jnp.arange(devices, dtype=jnp.int32)
    my_src = lax.dynamic_index_in_dim(src_all, own_index, 0, keepdims=False)
    my_rank = lax.dynamic_index_in_dim(rank_all, own_index, 0, keepdims=False)
    pick = (my_src[None, None, :] == band_range[:, None, None]) & (
        my_rank[None, None, :] == cap_range[None, :, None]
    )
    slot_of = jnp.sum(jnp.where(pick, order[None, None, :], 0), axis=2)
    has_slot = jnp.any(pick, axis=2)
    prints_flat = footprint.reshape(slot_count, footprint.shape[2])
    prints_laid = jnp.where(has_slot[:, :, None], prints_flat[slot_of], jnp.zeros((), jnp.bfloat16))
    chosen = (src_all[:, None, :] == own_index) & (rank_all[:, None, :] == cap_range[None, :, None])
    send_loc = jnp.sum(jnp.where(chosen, loc_all[:, None, :], 0), axis=2)
    filled = jnp.any(chosen, axis=2)
    outgoing = jnp.where(filled[:, :, None, None], tiles[send_loc], jnp.zeros((), jnp.bfloat16))
    arrived = lax.all_to_all(outgoing, "station", split_axis=0, concat_axis=0, tiled=True)
    slot_value = jnp.einsum(
        "ncst,nct->ncs", arrived, prints_laid, preferred_element_type=jnp.float32
    )
    live = (order % KT < tile_count[order // KT]).astype(jnp.float32)
    assign = pick.astype(jnp.float32) * live[None, None, :]
    station_hot = (
        (order // KT)[None, :] == jnp.arange(stations_here, dtype=jnp.int32)[:, None]
    ).astype(jnp.float32)
    weights = jnp.einsum("aj,dcj->adc", station_hot, assign, precision=lax.Precision.HIGHEST)
    observed = jnp.dot(
        weights.reshape(stations_here, devices * cap_slots),
        slot_value.reshape(devices * cap_slots, samples_here),
        precision=lax.Precision.HIGHEST,
        preferred_element_type=jnp.float32,
    )
    return lax.all_gather(observed, "sample", axis=1, tiled=True)


def solution(mesh):
    in_specs = (
        P("sample", "station", None),
        P("station", None),
        P("sample"),
        P("station", None, None),
        P(),
        P(),
        P("station"),
    )
    out_specs = P("station", None)
    return jax.shard_map(body, mesh=mesh, in_specs=in_specs, out_specs=out_specs, check_vma=False)
```

profile of v0, /device:TPU:0, one launch (start us, length us, event | category | flops | bytes accessed | tf_op | source)
XLA Modules:
  0.0 538.6 jit_solution(2112375514380005690)
XLA Ops:
  0.0 1.5 copy.53
  1.5 1.9 copy_convert_fusion
  4.1 2.4 collective-permute-start
  6.5 1.4 collective-permute-start.1
  8.0 2.8 fusion.81
  13.8 5.6 %fusion.8 = f32[4,32,3584]{2,0,1:T(4,128)S(1)} fusion(f32[4,32,3584]{2,0,1:T(4,128)S(1)} %copy_convert_fusion, f32[1,32,3584]{2,0,1:T(1,128)S(1)} %copy.53, f32[5,1,3584]{2,0,1:T(8,128)} %collective-permute-done.1, f32[5,1,3584]{2,0,1:T(8,128)S(1)} %collective-permute-done, f32[4,32,3583]{2,0,1:T(4,128)} %get-tuple-element.40, ...), kind=kLoop, calls=%fused_computation.32 | loop fusion | flops 6422528 | bytes 8400912 | tf_op jit(solution)/shard_map/add | solution.py:41
  20.5 5.1 collective-permute-start.2
  27.1 3.0 collective-permute-done.3
  30.1 4.7 fusion.15
  35.9 5.3 collective-permute-start.4
  41.2 1.5 collective-permute-start.5
  42.8 1.6 collective-permute-done.5
  44.5 4.7 fusion.22
  50.3 6.5 %collective-permute-start.6 = (f32[5,1,3584]{2,0,1:T(8,128)S(1)}, f32[5,1,3584]{2,0,1:T(8,128)S(1)}, u32[]{:S(2)}, u32[]{:S(2)}) collective-permute-start(f32[5,1,3584]{2,0,1:T(8,128)S(1)} %get-tuple-element.25), channel_id=1, source_target_pairs={{0,1},{1,2},{2,3},{3,4},{4,5},{5,6},{6,7},{7,8},{8,9},{9,10},{10,1... | collective-permute-start | bytes 215048 | tf_op jit(solution)/shard_map/ppermute | solution.py:20
  58.2 1.8 collective-permute-done.7
  60.0 4.7 fusion.29
  65.8 5.7 %collective-permute-start.8 = (f32[5,1,3584]{2,0,1:T(8,128)S(1)}, f32[5,1,3584]{2,0,1:T(8,128)S(1)}, u32[]{:S(2)}, u32[]{:S(2)}) collective-permute-start(f32[5,1,3584]{2,0,1:T(8,128)S(1)} %get-tuple-element.19), channel_id=1, source_target_pairs={{0,1},{1,2},{2,3},{3,4},{4,5},{5,6},{6,7},{7,8},{8,9},{9,10},{10,1... | collective-permute-start | bytes 215048 | tf_op jit(solution)/shard_map/ppermute | solution.py:20
  72.9 1.8 collective-permute-done.9
  74.8 4.7 fusion.36
  80.6 5.7 %collective-permute-start.10 = (f32[5,1,3584]{2,0,1:T(8,128)S(1)}, f32[5,1,3584]{2,0,1:T(8,128)S(1)}, u32[]{:S(2)}, u32[]{:S(2)}) collective-permute-start(f32[5,1,3584]{2,0,1:T(8,128)S(1)} %get-tuple-element.9), channel_id=1, source_target_pairs={{0,1},{1,2},{2,3},{3,4},{4,5},{5,6},{6,7},{7,8},{8,9},{9,10},{10,1... | collective-permute-start | bytes 215048 | tf_op jit(solution)/shard_map/ppermute | solution.py:20
  86.3 1.5 collective-permute-start.11
  87.9 1.6 collective-permute-done.11
  89.5 4.7 fusion.50
  96.1 16.6 %gather_fusion.1 = bf16[128,4,16384]{2,1,0:T(4,128)(2,1)} fusion(bf16[7,4,16384]{2,1,0:T(4,128)(2,1)S(1)} %reshape.208, s32[1024]{0:T(1024)S(1)} %pad_clamp_fusion.1), kind=kCustom, calls=%fused_computation.1 | custom fusion | bytes 33554944 | tf_op jit(solution)/shard_map/gather | solution.py:80
  112.7 12.2 %broadcast_select_fusion = bf16[32,4,4,16384]{3,2,1,0:T(4,128)(2,1)} fusion(bf16[32,4,4,16384]{3,2,1,0:T(4,128)(2,1)} %bitcast.36, pred[32,4]{1,0:T(8,128)(4,1)S(1)} %copy.51), kind=kLoop, calls=%fused_computation.3 | loop fusion | flops 8388608 | bytes 33554560 | tf_op jit(solution)/shard_map/jit(_where)/select_n | solution.py:80
  124.9 14.9 %all-to-all-start = ((bf16[32,4,4,16384]{3,2,1,0:T(4,128)(2,1)}), bf16[32,4,4,16384]{3,2,1,0:T(4,128)(2,1)}, u32[]{:S(2)}, u32[]{:S(2)}) async-start(bf16[32,4,4,16384]{3,2,1,0:T(4,128)(2,1)} %broadcast_select_fusion), calls=%async_computation | async-start | bytes 33554432 | tf_op jit(solution)/shard_map/all_to_all | solution.py:81
  140.2 2.6 reshape.209
  142.8 5.3 gather_fusion.2
  148.0 7.2 %reshape.227 = bf16[32,4,16384]{2,1,0:T(4,128)(2,1)} reshape(bf16[128,16384]{1,0:T(8,128)(2,1)} %gather_fusion.2) | data formatting | bytes 8388608 | tf_op jit(solution)/shard_map/gather | solution.py:76
  156.5 6.0 %select_bitcast_fusion = bf16[32,4,16384,1]{2,1,0,3:T(4,128)(2,1)} fusion(bf16[32,4,16384]{2,1,0:T(4,128)(2,1)} %reshape.227, pred[32,4]{1,0:T(8,128)(4,1)S(1)} %copy.63), kind=kLoop, calls=%fused_computation.6 | loop fusion | flops 2097152 | bytes 8388736 | tf_op jit(solution)/shard_map/jit(_where)/select_n | solution.py:76
  162.5 350.0 %all-to-all-done = bf16[32,4,4,16384]{3,2,1,0:T(4,128)(2,1)} async-done(((bf16[32,4,4,16384]{3,2,1,0:T(4,128)(2,1)}), bf16[32,4,4,16384]{3,2,1,0:T(4,128)(2,1)}, u32[]{:S(2)}, u32[]{:S(2)}) %all-to-all-start) | async-done | bytes 16777248 | tf_op jit(solution)/shard_map/all_to_all | solution.py:81
  512.5 25.3 %fusion = f32[32,4,1,4]{3,2,1,0:T(1,128)S(1)} fusion(bf16[32,4,4,16384]{3,2,1,0:T(4,128)(2,1)} %all-to-all-done, bf16[32,4,16384,1]{2,1,0,3:T(4,128)(2,1)} %select_bitcast_fusion), kind=kOutput, calls=%fused_computation.4 | convolution fusion | flops 16777216 | bytes 20973568 | tf_op jit(solution)/shard_map/ncst,nct->ncs/dot_general | solution.py:82
  (79 shorter events, 17.9 us)
Async XLA Ops:
  0.0 155.5 %copy-start = (s32[16]{0:T(128)S(1)}, s32[16]{0:T(128)}, u32[]{:S(2)}) copy-start(s32[16]{0:T(128)} %param.13) | copy-start | bytes 196
  4.1 9.6 %collective-permute-start = (f32[5,1,3584]{2,0,1:T(8,128)}, f32[5,1,3584]{2,0,1:T(8,128)S(1)}, u32[]{:S(2)}, u32[]{:S(2)}) collective-permute-start(f32[5,1,3584]{2,0,1:T(8,128)} %get-tuple-element.5), channel_id=1, source_target_pairs={{0,1},{1,2},{2,3},{3,4},{4,5},{5,6},{6,7},{7,8},{8,9},{9,10},{10,1... | collective-permute-start | bytes 215048 | tf_op jit(solution)/shard_map/ppermute | solution.py:20
  6.5 4.4 copy-start.7
  6.5 5.0 copy-start.2
  6.5 6.3 %copy-start.3 = (s32[512,4]{0,1:T(4,128)S(1)}, s32[512,4]{0,1:T(4,128)}, u32[]{:S(2)}) copy-start(s32[512,4]{0,1:T(4,128)} %param.12) | copy-start | bytes 24580
  6.5 7.2 %collective-permute-start.1 = (f32[5,1,3584]{2,0,1:T(8,128)}, f32[5,1,3584]{2,0,1:T(8,128)}, u32[]{:S(2)}, u32[]{:S(2)}) collective-permute-start(f32[5,1,3584]{2,0,1:T(8,128)} %get-tuple-element.43), channel_id=1, source_target_pairs={{1,0},{2,1},{3,2},{4,3},{5,4},{6,5},{7,6},{8,7},{9,8},{10,9},{11,1... | collective-permute-start | bytes 215048 | tf_op jit(solution)/shard_map/ppermute | solution.py:22
  10.8 3.0 copy-start.1
  20.5 9.7 %copy-start.6 = (f32[4]{0:T(128)S(1)}, f32[4]{0:T(128)}, u32[]{:S(2)}) copy-start(f32[4]{0:T(128)} %get-tuple-element.48) | copy-start | bytes 52
  20.5 6.5 %collective-permute-start.2 = (f32[5,1,3584]{2,0,1:T(8,128)S(1)}, f32[5,1,3584]{2,0,1:T(8,128)S(1)}, u32[]{:S(2)}, u32[]{:S(2)}) collective-permute-start(f32[5,1,3584]{2,0,1:T(8,128)S(1)} %get-tuple-element.37), channel_id=1, source_target_pairs={{0,1},{1,2},{2,3},{3,4},{4,5},{5,6},{6,7},{7,8},{8,9},{9,10},{10,1... | collective-permute-start | bytes 215048 | tf_op jit(solution)/shard_map/ppermute | solution.py:20
  25.7 4.5 collective-permute-start.3
  35.9 8.6 %copy-start.5 = (f32[4]{0:T(128)S(1)}, f32[4]{0:T(128)}, u32[]{:S(2)}) copy-start(f32[4]{0:T(128)} %get-tuple-element.47) | copy-start | bytes 52
  35.9 6.9 %collective-permute-start.4 = (f32[5,1,3584]{2,0,1:T(8,128)S(1)}, f32[5,1,3584]{2,0,1:T(8,128)S(1)}, u32[]{:S(2)}, u32[]{:S(2)}) collective-permute-start(f32[5,1,3584]{2,0,1:T(8,128)S(1)} %get-tuple-element.31), channel_id=1, source_target_pairs={{0,1},{1,2},{2,3},{3,4},{4,5},{5,6},{6,7},{7,8},{8,9},{9,10},{10,1... | collective-permute-start | bytes 215048 | tf_op jit(solution)/shard_map/ppermute | solution.py:20
  41.2 3.2 collective-permute-start.5
  50.2 9.8 %copy-start.4 = (f32[4]{0:T(128)S(1)}, f32[4]{0:T(128)}, u32[]{:S(2)}) copy-start(f32[4]{0:T(128)} %get-tuple-element.46) | copy-start | bytes 52
  50.3 7.9 %collective-permute-start.6 = (f32[5,1,3584]{2,0,1:T(8,128)S(1)}, f32[5,1,3584]{2,0,1:T(8,128)S(1)}, u32[]{:S(2)}, u32[]{:S(2)}) collective-permute-start(f32[5,1,3584]{2,0,1:T(8,128)S(1)} %get-tuple-element.25), channel_id=1, source_target_pairs={{0,1},{1,2},{2,3},{3,4},{4,5},{5,6},{6,7},{7,8},{8,9},{9,10},{10,1... | collective-permute-start | bytes 215048 | tf_op jit(solution)/shard_map/ppermute | solution.py:20
  56.8 3.2 collective-permute-start.7
  65.8 7.1 %collective-permute-start.8 = (f32[5,1,3584]{2,0,1:T(8,128)S(1)}, f32[5,1,3584]{2,0,1:T(8,128)S(1)}, u32[]{:S(2)}, u32[]{:S(2)}) collective-permute-start(f32[5,1,3584]{2,0,1:T(8,128)S(1)} %get-tuple-element.19), channel_id=1, source_target_pairs={{0,1},{1,2},{2,3},{3,4},{4,5},{5,6},{6,7},{7,8},{8,9},{9,10},{10,1... | collective-permute-start | bytes 215048 | tf_op jit(solution)/shard_map/ppermute | solution.py:20
  71.5 3.2 collective-permute-start.9
  80.6 7.3 %collective-permute-start.10 = (f32[5,1,3584]{2,0,1:T(8,128)S(1)}, f32[5,1,3584]{2,0,1:T(8,128)S(1)}, u32[]{:S(2)}, u32[]{:S(2)}) collective-permute-start(f32[5,1,3584]{2,0,1:T(8,128)S(1)} %get-tuple-element.9), channel_id=1, source_target_pairs={{0,1},{1,2},{2,3},{3,4},{4,5},{5,6},{6,7},{7,8},{8,9},{9,10},{10,1... | collective-permute-start | bytes 215048 | tf_op jit(solution)/shard_map/ppermute | solution.py:20
  86.3 3.2 collective-permute-start.11
  124.9 387.6 %all-to-all-start = ((bf16[32,4,4,16384]{3,2,1,0:T(4,128)(2,1)}), bf16[32,4,4,16384]{3,2,1,0:T(4,128)(2,1)}, u32[]{:S(2)}, u32[]{:S(2)}) async-start(bf16[32,4,4,16384]{3,2,1,0:T(4,128)(2,1)} %broadcast_select_fusion), calls=%async_computation | async-start | bytes 33554432 | tf_op jit(solution)/shard_map/all_to_all | solution.py:81
where the time goes:
time: 540 us; the launch traced here: 539 us
  waiting for transfers between devices  360 us (67%)
  starting transfers between devices  53.9 us (10%)
  other arithmetic  52.3 us (10%)
  local copies, waits for them, and re-layouts  45.8 us (8%)
  matrix products  26.3 us (5%)
    all_to_all x1, waiting for transfers between devices, body(): lax.all_to_all(outgoing, 'station', split_axis=0, concat_axis=0, tiled=True)  350 us
    ppermute x6, starting transfers between devices, extended_2(): lax.ppermute(tail, axis, [(i, (i + 1) % count) for i in range(ends)])  30.7 us
    dot_general x1, matrix products, body(): jnp.einsum('ncst,nct->ncs', arrived, prints_laid, preferred_element_type=...  25.3 us
    add x5, other arithmetic, diffuse_rows(): return (center + update, coefs[1:-1])  24.4 us
    gather x1, local copies, waits for them, and re-layouts, body(): tiles[send_loc]  16.6 us
    all_to_all x1, starting transfers between devices, body(): lax.all_to_all(outgoing, 'station', split_axis=0, concat_axis=0, tiled=True)  14.9 us
    gather x2, local copies, waits for them, and re-layouts, body(): prints_flat[slot_of]  12.4 us
    select_n x1, other arithmetic, body(): jnp.where(filled[:, :, None, None], tiles[send_loc], jnp.zeros((), jnp.bf...  12.2 us
  transfers between devices with their start and end apart: 13, of which 6 were waited for; matrix products, arithmetic and copies ran while one was open for 5% of the time, Pallas kernels for 0%

commit v1 on v0

v1 whole, which is shorter than its diff:
```python
import functools

import jax
import jax.numpy as jnp
from jax import lax
from jax.experimental import pallas as pl
from jax.experimental.pallas import tpu as pltpu
from jax.sharding import PartitionSpec as P

TILE_LON = 512
TILES_DEV = 7
LANES_T = 8
KT = 4
ITERS = 6
INNER = 8
CHUNKS = 4
MESH = pl.DeviceIdType.MESH


def east_west(x, lane, tile):
    width = x.shape[1]
    west = pltpu.roll(x, 1, 1)
    first = west[:, :128]
    before = jnp.where(tile == 0, pltpu.roll(first, 2, 0), pltpu.roll(first, 1, 0))
    first = jnp.where(lane == 0, before, first)
    west = jnp.concatenate([first, west[:, 128:]], axis=1)
    east = pltpu.roll(x, width - 1, 1)
    last = east[:, width - 128 :]
    after = jnp.where(tile == TILES_DEV - 1, pltpu.roll(last, 6, 0), pltpu.roll(last, 7, 0))
    last = jnp.where(lane == 127, after, last)
    east = jnp.concatenate([east[:, : width - 128], last], axis=1)
    return west, east


def kernel(
    outer_n, slots,
    gates, prints, hot, flux, coef, sel, group, weights,
    out,
    send, arr, halo_f, halo_c, field_a, field_b, cof, tiles, val, ret,
    f_send, f_recv, h_send, h_recv, r_send, r_recv, l_send, l_recv, v_send, v_recv,
):
    rows = flux.shape[0]
    wide = flux.shape[1]
    samples = wide // LANES_T
    count = outer_n * INNER
    me = lax.axis_index("station")
    outer, inner = me // INNER, lax.rem(me, INNER)
    base = outer * INNER
    has_up, has_down = me > 0, me < count - 1
    has_left, has_right = outer > 0, outer < outer_n - 1
    far_up = jnp.logical_and(has_up, inner == 0)
    far_down = jnp.logical_and(has_down, inner == INNER - 1)

    def peer(offset):
        return base + lax.rem(inner + offset, INNER)

    barrier = pltpu.get_barrier_semaphore()

    def greet(device):
        pl.semaphore_signal(barrier, inc=1, device_id={"station": device}, device_id_type=MESH)

    for offset in range(1, INNER):
        greet(peer(offset))
    others = ((has_left, -INNER), (has_right, INNER), (far_up, -1), (far_down, 1))
    for there, step in others:
        @pl.when(there)
        def _():
            greet(me + step)
    pl.semaphore_wait(barrier, INNER - 1 + sum(jnp.where(there, 1, 0) for there, _ in others))

    def remote(src, dst, ssem, rsem, device):
        return pltpu.make_async_remote_copy(
            src_ref=src, dst_ref=dst, send_sem=ssem, recv_sem=rsem,
            device_id={"station": device}, device_id_type=MESH,
        )

    def halo_copies(way):
        step = -1 if way == 0 else 1
        cut = pl.ds(0, ITERS) if way == 0 else pl.ds(rows - ITERS, ITERS)
        return (
            remote(flux.at[cut], halo_f.at[1 - way], h_send.at[way, 0], h_recv.at[1 - way, 0], me + step),
            remote(coef.at[cut], halo_c.at[1 - way], h_send.at[way, 1], h_recv.at[1 - way, 1], me + step),
        )

    for way, there in ((0, has_up), (1, has_down)):
        @pl.when(there)
        def _():
            for copy in halo_copies(way):
                copy.start()

        @pl.when(jnp.logical_not(there))
        def _():
            halo_f[way] = jnp.zeros(halo_f.shape[1:], halo_f.dtype)
            halo_c[way] = jnp.zeros(halo_c.shape[1:], halo_c.dtype)

    length = prints.shape[1] // CHUNKS

    def print_copy(offset, c):
        target = peer(offset)
        lanes = pl.ds(c * length, length)
        to_rows = pl.ds(pl.multiple_of(lax.rem(inner + offset, INNER) * slots, slots), slots)
        my_rows = pl.ds(pl.multiple_of(inner * slots, slots), slots)
        return remote(send.at[to_rows, lanes], arr.at[my_rows, lanes], f_send.at[offset, c], f_recv.at[offset, c], target)

    for c in range(CHUNKS):
        def pack(i, carry):
            lanes = pl.ds(pl.multiple_of(c * length + i * 512, 512), 512)
            send[:, lanes] = jnp.dot(hot[...], prints[:, lanes], preferred_element_type=jnp.float32).astype(jnp.bfloat16)
            return carry

        lax.fori_loop(0, length // 512, pack, 0)
        for offset in range(1, INNER):
            print_copy(offset, c).start()
    own = pl.ds(pl.multiple_of(inner * slots, slots), slots)
    arr[own, :] = send[own, :]

    def load(r, carry):
        field_a[r + ITERS] = flux[r].astype(jnp.float32)
        cof[r + ITERS] = coef[r]
        return carry

    lax.fori_loop(0, rows, load, 0)
    for way, there in ((0, has_up), (1, has_down)):
        @pl.when(there)
        def _():
            for copy in halo_copies(way):
                copy.wait_send()
            remote(flux.at[pl.ds(0, ITERS)], halo_f.at[way], h_send.at[way, 0], h_recv.at[way, 0], me).wait_recv()
            remote(coef.at[pl.ds(0, ITERS)], halo_c.at[way], h_send.at[way, 1], h_recv.at[way, 1], me).wait_recv()

    def load_halo(r, carry):
        field_a[r] = halo_f[0, r].astype(jnp.float32)
        cof[r] = halo_c[0, r]
        field_a[r + ITERS + rows] = halo_f[1, r].astype(jnp.float32)
        cof[r + ITERS + rows] = halo_c[1, r]
        return carry

    lax.fori_loop(0, ITERS, load_halo, 0)

    lane = lax.broadcasted_iota(jnp.int32, (LANES_T, 128), 1)
    tile = lax.broadcasted_iota(jnp.int32, (LANES_T, 128), 0)

    def updated(src, r, k, s):
        cut = slice(s * LANES_T, (s + 1) * LANES_T)
        center = src[r, cut, :]
        west, east = east_west(center, lane, tile)
        lap = src[r - 1, cut, :] + src[r + 1, cut, :] + west + east - 4.0 * center
        return center + gates[k, s] * cof[r] * lap

    src, dst = field_a, field_b
    for k in range(ITERS - 1):
        def one_row(r, carry, src=src, dst=dst, k=k):
            for s in range(samples):
                dst[r, s * LANES_T : (s + 1) * LANES_T, :] = updated(src, r, k, s)
            return carry

        lax.fori_loop(k + 1, rows + 2 * ITERS - 1 - k, one_row, 0)
        src, dst = dst, src

    piece = rows // CHUNKS

    def block_copy(block, c, k, to_right):
        at = tiles.at[pl.ds(c * piece, piece), pl.ds(pl.multiple_of(block * wide, wide), wide), :]
        if to_right:
            return remote(at, at, r_send.at[k, c], r_recv.at[k, c], me + INNER)
        return remote(at, at, l_send.at[k, c], l_recv.at[k, c], me - INNER)

    def start_block(block, c, k, to_right, there):
        @pl.when(jnp.logical_and(there, has_right if to_right else has_left))
        def _():
            block_copy(block, c, k, to_right).start()

    mine = pl.ds(pl.multiple_of(outer * wide, wide), wide)
    for c in range(CHUNKS):
        def last_row(r, carry, src=src):
            done = [updated(src, r + ITERS, ITERS - 1, s) for s in range(samples)]
            tiles[r, mine, :] = jnp.concatenate(done, axis=0).astype(jnp.bfloat16)
            return carry

        lax.fori_loop(c * piece, (c + 1) * piece, last_row, 0)
        start_block(outer, c, 0, True, has_right)
        start_block(outer, c, 0, False, has_left)

    acc = jnp.zeros((INNER * slots, outer_n * wide), jnp.float32)
    for k in range(outer_n - 1):
        for c in range(CHUNKS):
            from_left, from_right = outer - 1 - k >= 0, outer + 1 + k < outer_n

            @pl.when(from_left)
            def _():
                block_copy(outer - 1 - k, c, k, True).wait_recv()

            if k < outer_n - 2:
                start_block(outer - 1 - k, c, k + 1, True, from_left)

            @pl.when(from_right)
            def _():
                block_copy(outer + 1 + k, c, k, False).wait_recv()

            if k < outer_n - 2:
                start_block(outer + 1 + k, c, k + 1, False, from_right)

            if k == outer_n - 2:
                for offset in range(1, INNER):
                    print_copy(offset, c).wait_recv()

                def multiply(r, total):
                    lanes = pl.ds(pl.multiple_of(r * TILE_LON, TILE_LON), TILE_LON)
                    return total + lax.dot_general(
                        arr[:, lanes], tiles[r], (((1,), (1,)), ((), ())),
                        preferred_element_type=jnp.float32,
                    )

                acc = lax.fori_loop(c * piece, (c + 1) * piece, multiply, acc)

    val[...] = jnp.dot(acc * sel[...], group[...], precision=lax.Precision.HIGHEST, preferred_element_type=jnp.float32)

    def value_copy(offset):
        to_rows = pl.ds(pl.multiple_of(lax.rem(inner + offset, INNER) * slots, slots), slots)
        return remote(val.at[to_rows], ret.at[own], v_send.at[offset], v_recv.at[offset], peer(offset))

    for offset in range(1, INNER):
        value_copy(offset).start()
    ret[own, :] = val[own, :]
    for offset in range(1, INNER):
        value_copy(offset).wait_recv()
    out[...] = jnp.dot(weights[...], ret[...], precision=lax.Precision.HIGHEST, preferred_element_type=jnp.float32)

    for offset in range(1, INNER):
        value_copy(offset).wait_send()
        for c in range(CHUNKS):
            print_copy(offset, c).wait_send()
    for k in range(outer_n - 1):
        for c in range(CHUNKS):
            @pl.when(jnp.logical_and(outer - k >= 0, has_right))
            def _():
                block_copy(outer - k, c, k, True).wait_send()

            @pl.when(jnp.logical_and(outer + k < outer_n, has_left))
            def _():
                block_copy(outer + k, c, k, False).wait_send()


def body(flux, coeff, diff_steps, footprint, tile_src, tile_local, tile_count):
    samples, rows, _ = flux.shape
    stations = footprint.shape[0]
    devices = lax.axis_size("station")
    outer_n = devices // INNER
    me = lax.axis_index("station")
    outer, inner = me // INNER, me % INNER
    slot_count = stations * KT
    cap = 2 * max(1, (slot_count + devices - 1) // devices)
    slots = outer_n * cap
    wide = samples * LANES_T

    flux_t = flux.reshape(samples, rows, TILES_DEV, TILE_LON).transpose(1, 0, 2, 3)
    flux_t = jnp.pad(flux_t, ((0, 0), (0, 0), (0, 1), (0, 0))).reshape(rows, wide, TILE_LON)
    coef_t = jnp.pad(coeff.reshape(rows, TILES_DEV, TILE_LON), ((0, 0), (0, 1), (0, 0)))
    gates = (jnp.arange(ITERS, dtype=jnp.int32)[:, None] < diff_steps[None, :]).astype(jnp.float32)

    order = jnp.arange(slot_count, dtype=jnp.int32)
    src = lax.dynamic_slice_in_dim(tile_src.reshape(devices, slot_count), outer * INNER, INNER, 0)
    loc = lax.dynamic_slice_in_dim(tile_local.reshape(devices, slot_count), outer * INNER, INNER, 0)
    target = src % INNER
    same = (target[:, :, None] == target[:, None, :]) & (order[None, :] < order[:, None])[None]
    rank = jnp.sum(same.astype(jnp.int32), axis=2)
    places = jnp.arange(slots, dtype=jnp.int32)
    my_target = lax.dynamic_index_in_dim(target, inner, 0, keepdims=False)
    my_rank = lax.dynamic_index_in_dim(rank, inner, 0, keepdims=False)
    place = my_target * slots + my_rank
    hot = place[None, :] == jnp.arange(INNER * slots, dtype=jnp.int32)[:, None]
    chosen = (target[:, None, :] == inner) & (rank[:, None, :] == places[None, :, None])
    code = (src // INNER) * LANES_T + loc + 1
    named = jnp.sum(jnp.where(chosen, code[:, None, :], 0), axis=2).reshape(INNER * slots) - 1
    columns = jnp.arange(outer_n * wide, dtype=jnp.int32)
    column_code = (columns // wide) * LANES_T + columns % LANES_T
    sel = (named[:, None] == column_code[None, :]).astype(jnp.float32)
    group = ((columns % wide) // LANES_T)[:, None] == jnp.arange(128, dtype=jnp.int32)[None, :]
    live = order % KT < tile_count[order // KT]
    mine = (order // KT)[None, :] == jnp.arange(stations, dtype=jnp.int32)[:, None]
    hits = (mine & live[None, :])[:, :, None] & (place[None, :, None] == jnp.arange(INNER * slots, dtype=jnp.int32)[None, None, :])
    weights = jnp.sum(hits.astype(jnp.float32), axis=1)

    ext = rows + 2 * ITERS
    vmem = pl.BlockSpec(memory_space=pltpu.VMEM)
    dma = pltpu.SemaphoreType.DMA
    observed = pl.pallas_call(
        functools.partial(kernel, outer_n, slots),
        out_shape=jax.ShapeDtypeStruct((stations, 128), jnp.float32),
        in_specs=[pl.BlockSpec(memory_space=pltpu.SMEM)] + [vmem] * 7,
        out_specs=vmem,
        scratch_shapes=[
            pltpu.VMEM((INNER * slots, footprint.shape[2]), jnp.bfloat16),
            pltpu.VMEM((INNER * slots, footprint.shape[2]), jnp.bfloat16),
            pltpu.VMEM((2, ITERS, wide, TILE_LON), jnp.bfloat16),
            pltpu.VMEM((2, ITERS, LANES_T, TILE_LON), jnp.float32),
            pltpu.VMEM((ext, wide, TILE_LON), jnp.float32),
            pltpu.VMEM((ext, wide, TILE_LON), jnp.float32),
            pltpu.VMEM((ext, LANES_T, TILE_LON), jnp.float32),
            pltpu.VMEM((rows, outer_n * wide, TILE_LON), jnp.bfloat16),
            pltpu.VMEM((INNER * slots, 128), jnp.float32),
            pltpu.VMEM((INNER * slots, 128), jnp.float32),
            dma((INNER, CHUNKS)), dma((INNER, CHUNKS)),
            dma((2, 2)), dma((2, 2)),
            dma((outer_n - 1, CHUNKS)), dma((outer_n - 1, CHUNKS)),
            dma((outer_n - 1, CHUNKS)), dma((outer_n - 1, CHUNKS)),
            dma((INNER,)), dma((INNER,)),
        ],
        compiler_params=pltpu.CompilerParams(
            collective_id=0, has_side_effects=True, vmem_limit_bytes=48 * 1024 * 1024
        ),
    )(
        gates, footprint.reshape(slot_count, footprint.shape[2]), hot.astype(jnp.bfloat16),
        flux_t, coef_t, sel, group.astype(jnp.float32), weights,
    )
    return lax.all_gather(observed[:, :samples], "sample", axis=1, tiled=True)


def solution(mesh):
    in_specs = (
        P("sample", "station", None),
        P("station", None),
        P("sample"),
        P("station", None, None),
        P(),
        P(),
        P("station"),
    )
    out_specs = P("station", None)
    return jax.shard_map(body, mesh=mesh, in_specs=in_specs, out_specs=out_specs, check_vma=False)
```

time: 540 us -> 123 us (0.23)
  waiting for transfers between devices: 360 us -> 0 us
  Pallas kernels: 0 us -> 111 us
  starting transfers between devices: 53.9 us -> 0 us
  other arithmetic: 52.3 us -> 1.78 us
  local copies, waits for them, and re-layouts: 45.8 us -> 10 us
  matrix products: 26.3 us -> 0 us
    all_to_all x1 -> x0, waiting for transfers between devices: 350 us -> none  [body(): lax.all_to_all(outgoing, 'station', split_axis=0, concat_axis=0, tiled=True)]
    pallas_call x0 -> x1, Pallas kernels: none -> 111 us  [body(): pl.pallas_call(functools.partial(kernel, outer_n, slots), out_shape=jax.S...]
    ppermute x12 -> x0, starting transfers between devices: 39 us -> none  [the longest x6 30.7 us: extended_2(): lax.ppermute(tail, axis, [(i, (i + 1) % count) for i in range(ends)])]
    gather x4 -> x1, local copies, waits for them, and re-layouts: 29.8 us -> 0.77 us  [body(): live = order % KT < tile_count[order // KT]]
    dot_general x3 -> x0, matrix products: 26.3 us -> none  [the longest x1 25.3 us: body(): jnp.einsum('ncst,nct->ncs', arrived, prints_laid, preferred_element_type=...]
    add x5 -> x1, other arithmetic: 24.4 us -> 0.02 us  [body(): code = src // INNER * LANES_T + loc + 1]
    select_n x5 -> x2, other arithmetic: 18.2 us -> 0.02 us  [the longest x1 0.01 us: body(): live = order % KT < tile_count[order // KT]]
    all_to_all x1 -> x0, starting transfers between devices: 14.9 us -> none  [body(): lax.all_to_all(outgoing, 'station', split_axis=0, concat_axis=0, tiled=True)]
  transfers between devices with their start and end apart: 13 -> 0, of which waited for: 6 -> 0; matrix products, arithmetic and copies ran while one was open for 5% -> 0% of each run, Pallas kernels for 0% -> 0%
where the time goes in v1:
time: 123 us; the launch traced here: 122 us
  Pallas kernels  111 us (90%)
  local copies, waits for them, and re-layouts  10 us (8%)
  other arithmetic  1.78 us (1%)
    pallas_call x1, Pallas kernels, body(): pl.pallas_call(functools.partial(kernel, outer_n, slots), out_shape=jax.S...  111 us
    unnamed x10, local copies, waits for them, and re-layouts  3.32 us
    reshape x1, local copies, waits for them, and re-layouts, body(): footprint.reshape(slot_count, footprint.shape[2])  2.55 us

profile of v1, /device:TPU:0, one launch (start us, length us, event | category | flops | bytes accessed | tf_op | source)
XLA Modules:
  0.0 122.5 jit_solution(931057053069186445)
XLA Ops:
  0.0 0.0 copy-start
  0.0 0.0 copy-start.3
  0.0 0.0 copy-start.2
  0.1 0.6 copy-done
  0.7 0.8 gather_fusion
  1.5 0.7 fusion.7.gates
  2.1 0.1 fusion.2.group
  2.2 0.8 copy.14
  3.1 0.1 reshape.228
  3.2 0.3 convert_reduce_fusion.1
  3.6 0.1 iota_compare_fusion.3
  3.7 0.2 convert_reduce_fusion.weights
  3.9 0.8 copy.16
  4.8 0.1 reshape.232
  4.9 0.2 select_reduce_fusion
  5.2 0.1 sub.39
  5.2 0.1 compare_convert_fusion.sel
  5.3 0.0 copy-done.3
  5.3 0.2 reshape.231
  5.6 0.8 pad.9.coef
  6.4 0.0 copy-done.2
  6.4 1.0 reshape.229
  7.5 0.2 pad_bitcast_fusion.flux
  7.7 2.6 %reshape.227.prints = bf16[64,16384]{1,0:T(8,128)(2,1)S(1)} reshape(bf16[16,4,16384]{2,1,0:T(4,128)(2,1)} %param.10) | data formatting | bytes 4194304 | tf_op jit(solution)/shard_map/reshape | solution.py:313
  10.3 0.0 copy-start.1
  10.3 1.0 copy-done.1
  11.3 110.5 %shard_map.73 = f32[16,128]{1,0:T(8,128)S(1)} custom-call(f32[6,4]{1,0:T(8,128)S(1)} %fusion.7.gates, bf16[64,16384]{1,0:T(8,128)(2,1)S(1)} %reshape.227.prints, bf16[128,64]{1,0:T(8,128)(2,1)S(1)} %fusion.hot, bf16[32,32,512]{2,1,0:T(8,128)(2,1)S(1)} %pad_bitcast_fusion.flux, f32[32,8,512]{2,1,0:T(8,128)S(1)} %copy-done.1, ...), custom_call_target="tpu_custom_call" | custom-call | tf_op jit(solution)/shard_map/pallas_call | solution.py:287
  121.8 0.7 copy.17
  (12 shorter events, 0.1 us)
Async XLA Ops:
  0.0 0.7 copy-start
  0.0 5.3 %copy-start.3 = (f32[32,3584]{1,0:T(8,128)S(1)}, f32[32,3584]{1,0:T(8,128)}, u32[]{:S(2)}) copy-start(f32[32,3584]{1,0:T(8,128)} %param.8) | copy-start | bytes 1376260
  0.0 6.4 %copy-start.2 = (bf16[4,32,3584]{2,1,0:T(8,128)(2,1)S(1)}, bf16[4,32,3584]{2,1,0:T(8,128)(2,1)}, u32[]{:S(2)}) copy-start(bf16[4,32,3584]{2,1,0:T(8,128)(2,1)} %param.7) | copy-start | bytes 2752516
  10.3 1.0 copy-start.1

commit v2 on v1

--- a/solution.py
+++ b/solution.py
@@ -104,11 +104,12 @@
 
     for c in range(CHUNKS):
         def pack(i, carry):
-            lanes = pl.ds(pl.multiple_of(c * length + i * 512, 512), 512)
-            send[:, lanes] = jnp.dot(hot[...], prints[:, lanes], preferred_element_type=jnp.float32).astype(jnp.bfloat16)
+            for j in range(4):
+                lanes = pl.ds(pl.multiple_of(c * length + i * 1024 + j * 256, 256), 256)
+                send[:, lanes] = jnp.dot(hot[...], prints[:, lanes], preferred_element_type=jnp.float32).astype(jnp.bfloat16)
             return carry
 
-        lax.fori_loop(0, length // 512, pack, 0)
+        lax.fori_loop(0, length // 1024, pack, 0)
         for offset in range(1, INNER):
             print_copy(offset, c).start()
     own = pl.ds(pl.multiple_of(inner * slots, slots), slots)
@@ -149,12 +150,13 @@
 
     src, dst = field_a, field_b
     for k in range(ITERS - 1):
-        def one_row(r, carry, src=src, dst=dst, k=k):
-            for s in range(samples):
-                dst[r, s * LANES_T : (s + 1) * LANES_T, :] = updated(src, r, k, s)
+        def row_pair(i, carry, src=src, dst=dst, k=k):
+            for r in (k + 1 + 2 * i, k + 2 + 2 * i):
+                for s in range(samples):
+                    dst[r, s * LANES_T : (s + 1) * LANES_T, :] = updated(src, r, k, s)
             return carry
 
-        lax.fori_loop(k + 1, rows + 2 * ITERS - 1 - k, one_row, 0)
+        lax.fori_loop(0, rows // 2 + ITERS - 1 - k, row_pair, 0)
         src, dst = dst, src
 
     piece = rows // CHUNKS
@@ -172,12 +174,13 @@
 
     mine = pl.ds(pl.multiple_of(outer * wide, wide), wide)
     for c in range(CHUNKS):
-        def last_row(r, carry, src=src):
-            done = [updated(src, r + ITERS, ITERS - 1, s) for s in range(samples)]
-            tiles[r, mine, :] = jnp.concatenate(done, axis=0).astype(jnp.bfloat16)
+        def last_pair(i, carry, src=src):
+            for r in (c * piece + 2 * i, c * piece + 2 * i + 1):
+                done = [updated(src, r + ITERS, ITERS - 1, s) for s in range(samples)]
+                tiles[r, mine, :] = jnp.concatenate(done, axis=0).astype(jnp.bfloat16)
             return carry
 
-        lax.fori_loop(c * piece, (c + 1) * piece, last_row, 0)
+        lax.fori_loop(0, piece // 2, last_pair, 0)
         start_block(outer, c, 0, True, has_right)
         start_block(outer, c, 0, False, has_left)
 
@@ -204,14 +207,16 @@
                 for offset in range(1, INNER):
                     print_copy(offset, c).wait_recv()
 
-                def multiply(r, total):
-                    lanes = pl.ds(pl.multiple_of(r * TILE_LON, TILE_LON), TILE_LON)
-                    return total + lax.dot_general(
-                        arr[:, lanes], tiles[r], (((1,), (1,)), ((), ())),
-                        preferred_element_type=jnp.float32,
-                    )
-
-                acc = lax.fori_loop(c * piece, (c + 1) * piece, multiply, acc)
+                def multiply(i, total):
+                    for r in (c * piece + 2 * i, c * piece + 2 * i + 1):
+                        lanes = pl.ds(pl.multiple_of(r * TILE_LON, TILE_LON), TILE_LON)
+                        total = total + lax.dot_general(
+                            arr[:, lanes], tiles[r], (((1,), (1,)), ((), ())),
+                            preferred_element_type=jnp.float32,
+                        )
+                    return total
+
+                acc = lax.fori_loop(0, piece // 2, multiply, acc)
 
     val[...] = jnp.dot(acc * sel[...], group[...], precision=lax.Precision.HIGHEST, preferred_element_type=jnp.float32)
 

time: 123 us -> 115 us (0.935)
  Pallas kernels: 111 us -> 103 us
    pallas_call x1, Pallas kernels: 111 us -> 103 us  [body(): pl.pallas_call(functools.partial(kernel, outer_n, slots), out_shape=jax.S...]
where the time goes in v2:
time: 115 us
  Pallas kernels  103 us (90%)
  local copies, waits for them, and re-layouts  10 us (9%)
  other arithmetic  1.78 us (2%)
    pallas_call x1, Pallas kernels, body(): pl.pallas_call(functools.partial(kernel, outer_n, slots), out_shape=jax.S...  103 us
    unnamed x10, local copies, waits for them, and re-layouts  3.32 us
    reshape x1, local copies, waits for them, and re-layouts, body(): footprint.reshape(slot_count, footprint.shape[2])  2.55 us

profile of v2, /device:TPU:0, one launch (start us, length us, event | category | flops | bytes accessed | tf_op | source)
XLA Modules:
  0.0 115.1 jit_solution(3329375450271357584)
XLA Ops:
  0.0 0.0 copy-start
  0.0 0.0 copy-start.3
  0.0 0.0 copy-start.2
  0.1 0.6 copy-done
  0.7 0.8 gather_fusion
  1.5 0.7 fusion.7.gates
  2.1 0.1 fusion.2.group
  2.2 0.8 copy.14
  3.1 0.1 reshape.228
  3.2 0.3 convert_reduce_fusion.1
  3.6 0.1 iota_compare_fusion.3
  3.7 0.2 convert_reduce_fusion.weights
  3.9 0.8 copy.16
  4.8 0.1 reshape.232
  4.9 0.2 select_reduce_fusion
  5.2 0.1 sub.39
  5.2 0.1 compare_convert_fusion.sel
  5.3 0.0 copy-done.3
  5.3 0.2 reshape.231
  5.6 0.8 pad.9.coef
  6.4 0.0 copy-done.2
  6.4 1.0 reshape.229
  7.5 0.2 pad_bitcast_fusion.flux
  7.7 2.6 %reshape.227.prints = bf16[64,16384]{1,0:T(8,128)(2,1)S(1)} reshape(bf16[16,4,16384]{2,1,0:T(4,128)(2,1)} %param.10) | data formatting | bytes 4194304 | tf_op jit(solution)/shard_map/reshape | solution.py:318
  10.3 0.0 copy-start.1
  10.3 1.0 copy-done.1
  11.3 103.1 %shard_map.73 = f32[16,128]{1,0:T(8,128)S(1)} custom-call(f32[6,4]{1,0:T(8,128)S(1)} %fusion.7.gates, bf16[64,16384]{1,0:T(8,128)(2,1)S(1)} %reshape.227.prints, bf16[128,64]{1,0:T(8,128)(2,1)S(1)} %fusion.hot, bf16[32,32,512]{2,1,0:T(8,128)(2,1)S(1)} %pad_bitcast_fusion.flux, f32[32,8,512]{2,1,0:T(8,128)S(1)} %copy-done.1, ...), custom_call_target="tpu_custom_call" | custom-call | tf_op jit(solution)/shard_map/pallas_call | solution.py:292
  114.5 0.7 copy.17
  (12 shorter events, 0.1 us)
Async XLA Ops:
  0.0 0.7 copy-start
  0.0 5.3 %copy-start.3 = (f32[32,3584]{1,0:T(8,128)S(1)}, f32[32,3584]{1,0:T(8,128)}, u32[]{:S(2)}) copy-start(f32[32,3584]{1,0:T(8,128)} %param.8) | copy-start | bytes 1376260
  0.0 6.4 %copy-start.2 = (bf16[4,32,3584]{2,1,0:T(8,128)(2,1)S(1)}, bf16[4,32,3584]{2,1,0:T(8,128)(2,1)}, u32[]{:S(2)}) copy-start(bf16[4,32,3584]{2,1,0:T(8,128)(2,1)} %param.7) | copy-start | bytes 2752516
  10.3 1.0 copy-start.1

commit v3 on v2

--- a/solution.py
+++ b/solution.py
@@ -14,6 +14,8 @@
 ITERS = 6
 INNER = 8
 CHUNKS = 4
+PIECES = 8
+GROUP_ROWS = 16
 MESH = pl.DeviceIdType.MESH
 
 
@@ -33,11 +35,11 @@
 
 
 def kernel(
-    outer_n, slots,
-    gates, prints, hot, flux, coef, sel, group, weights,
+    outer_n, slots, splits,
+    gates, prints, hot, hot2, flux, coef, sel, sel2, group, weights, weights2,
     out,
-    send, arr, halo_f, halo_c, field_a, field_b, cof, tiles, val, ret,
-    f_send, f_recv, h_send, h_recv, r_send, r_recv, l_send, l_recv, v_send, v_recv,
+    send, arr, send2, arr2, halo_f, halo_c, field_a, field_b, cof, tiles, acc, val, ret, val2, ret2,
+    f_send, f_recv, g_send, g_recv, h_send, h_recv, r_send, r_recv, l_send, l_recv, v_send, v_recv, w_send, w_recv,
 ):
     rows = flux.shape[0]
     wide = flux.shape[1]
@@ -48,12 +50,21 @@
     base = outer * INNER
     has_up, has_down = me > 0, me < count - 1
     has_left, has_right = outer > 0, outer < outer_n - 1
-    far_up = jnp.logical_and(has_up, inner == 0)
-    far_down = jnp.logical_and(has_down, inner == INNER - 1)
+    first, last = outer == 0, outer == outer_n - 1
+    is_end = jnp.logical_or(first, last)
+    is_next = jnp.logical_or(outer == 1, outer == outer_n - 2)
+    other_base = jnp.where(first, 1, jnp.where(last, outer_n - 2, jnp.where(outer == 1, 0, outer_n - 1))) * INNER
+    lone_left = jnp.logical_and(outer >= 2, outer <= outer_n - 2)
+    lone_right = jnp.logical_and(outer >= 1, outer <= outer_n - 3)
+    lone_up = jnp.logical_and(lone_left, inner == 0)
+    lone_down = jnp.logical_and(lone_right, inner == INNER - 1)
 
     def peer(offset):
         return base + lax.rem(inner + offset, INNER)
 
+    def across(offset):
+        return other_base + lax.rem(inner + offset, INNER)
+
     barrier = pltpu.get_barrier_semaphore()
 
     def greet(device):
@@ -61,12 +72,22 @@
 
     for offset in range(1, INNER):
         greet(peer(offset))
-    others = ((has_left, -INNER), (has_right, INNER), (far_up, -1), (far_down, 1))
+    others = ((lone_left, -INNER), (lone_right, INNER), (lone_up, -1), (lone_down, 1))
     for there, step in others:
         @pl.when(there)
         def _():
             greet(me + step)
-    pl.semaphore_wait(barrier, INNER - 1 + sum(jnp.where(there, 1, 0) for there, _ in others))
+
+    paired = jnp.logical_or(is_end, is_next)
+
+    @pl.when(paired)
+    def _():
+        for offset in range(INNER):
+            greet(across(offset))
+    pl.semaphore_wait(
+        barrier,
+        INNER - 1 + sum(jnp.where(there, 1, 0) for there, _ in others) + jnp.where(paired, INNER, 0),
+    )
 
     def remote(src, dst, ssem, rsem, device):
         return pltpu.make_async_remote_copy(
@@ -92,6 +113,36 @@
         def _():
             halo_f[way] = jnp.zeros(halo_f.shape[1:], halo_f.dtype)
             halo_c[way] = jnp.zeros(halo_c.shape[1:], halo_c.dtype)
+
+    short = prints.shape[1] // splits
+    own2 = pl.ds(pl.multiple_of(inner * GROUP_ROWS, GROUP_ROWS), GROUP_ROWS)
+
+    def rows2(offset):
+        return pl.ds(pl.multiple_of(lax.rem(inner + offset, INNER) * GROUP_ROWS, GROUP_ROWS), GROUP_ROWS)
+
+    def group_copy(offset):
+        return remote(send2.at[rows2(offset)], arr2.at[own2], g_send.at[offset], g_recv.at[offset], across(offset))
+
+    @pl.when(is_end)
+    def _():
+        def pack2(i, carry):
+            for j in range(2):
+                at = i * 512 + j * 256
+                stack = [prints[:, pl.ds(pl.multiple_of(q * short + at, 256), 256)] for q in range(splits)]
+                packed = jnp.dot(hot2[...], jnp.concatenate(stack, axis=0), preferred_element_type=jnp.float32)
+                send2[:, pl.ds(pl.multiple_of(at, 256), 256)] = packed.astype(jnp.bfloat16)
+            return carry
+
+        lax.fori_loop(0, short // 512, pack2, 0)
+        for offset in range(INNER):
+            group_copy(offset).start()
+        missing = jnp.where(first, 1, outer_n - 2)
+
+        def clear(r, carry):
+            tiles[r, pl.ds(pl.multiple_of(missing * wide, wide), wide), :] = jnp.zeros((wide, TILE_LON), jnp.bfloat16)
+            return carry
+
+        lax.fori_loop(0, rows, clear, 0)
 
     length = prints.shape[1] // CHUNKS
 
@@ -159,7 +210,7 @@
         lax.fori_loop(0, rows // 2 + ITERS - 1 - k, row_pair, 0)
         src, dst = dst, src
 
-    piece = rows // CHUNKS
+    piece = rows // PIECES
 
     def block_copy(block, c, k, to_right):
         at = tiles.at[pl.ds(c * piece, piece), pl.ds(pl.multiple_of(block * wide, wide), wide), :]
@@ -167,13 +218,19 @@
             return remote(at, at, r_send.at[k, c], r_recv.at[k, c], me + INNER)
         return remote(at, at, l_send.at[k, c], l_recv.at[k, c], me - INNER)
 
+    def goes(there, k, to_right):
+        there = jnp.logical_and(there, has_right if to_right else has_left)
+        if k == 0:
+            there = jnp.logical_and(there, outer != (outer_n - 2 if to_right else 1))
+        return there
+
     def start_block(block, c, k, to_right, there):
-        @pl.when(jnp.logical_and(there, has_right if to_right else has_left))
+        @pl.when(goes(there, k, to_right))
         def _():
             block_copy(block, c, k, to_right).start()
 
     mine = pl.ds(pl.multiple_of(outer * wide, wide), wide)
-    for c in range(CHUNKS):
+    for c in range(PIECES):
         def last_pair(i, carry, src=src):
             for r in (c * piece + 2 * i, c * piece + 2 * i + 1):
                 done = [updated(src, r + ITERS, ITERS - 1, s) for s in range(samples)]
@@ -184,11 +241,48 @@
         start_block(outer, c, 0, True, has_right)
         start_block(outer, c, 0, False, has_left)
 
-    acc = jnp.zeros((INNER * slots, outer_n * wide), jnp.float32)
+    def multiply(c):
+        if c * CHUNKS % PIECES == 0:
+            for offset in range(1, INNER):
+                print_copy(offset, c * CHUNKS // PIECES).wait_recv()
+        total = jnp.zeros(acc.shape, jnp.float32) if c == 0 else acc[...]
+        for r in range(c * piece, (c + 1) * piece):
+            total = total + lax.dot_general(
+                arr[:, r * TILE_LON : (r + 1) * TILE_LON], tiles[r], (((1,), (1,)), ((), ())),
+                preferred_element_type=jnp.float32,
+            )
+        acc[...] = total
+
+    def value_copy2(offset):
+        return remote(val2.at[rows2(offset)], ret2.at[own2], w_send.at[offset], w_recv.at[offset], across(offset))
+
+    def group_values():
+        for offset in range(INNER):
+            group_copy(offset).wait_recv()
+        per_split = rows // splits
+        total = jnp.zeros(sel2.shape[1:], jnp.float32)
+        for q in range(splits):
+            def add_row(r, part, q=q):
+                return part + lax.dot_general(
+                    arr2[:, pl.ds(pl.multiple_of(r * TILE_LON, TILE_LON), TILE_LON)],
+                    tiles[q * per_split + r, mine, :], (((1,), (1,)), ((), ())),
+                    preferred_element_type=jnp.float32,
+                )
+
+            part = jnp.zeros(sel2.shape[1:], jnp.float32)
+            for r in range(per_split):
+                part = add_row(r, part)
+            total = total + part * sel2[q]
+        val2[...] = jnp.dot(total, group[:wide, :], precision=lax.Precision.HIGHEST, preferred_element_type=jnp.float32)
+        for offset in range(INNER):
+            value_copy2(offset).start()
+
     for k in range(outer_n - 1):
-        for c in range(CHUNKS):
-            from_left, from_right = outer - 1 - k >= 0, outer + 1 + k < outer_n
-
+        from_left, from_right = outer - 1 - k >= 0, outer + 1 + k < outer_n
+        if k == 0:
+            from_left = jnp.logical_and(from_left, jnp.logical_not(last))
+            from_right = jnp.logical_and(from_right, jnp.logical_not(first))
+        for c in range(PIECES):
             @pl.when(from_left)
             def _():
                 block_copy(outer - 1 - k, c, k, True).wait_recv()
@@ -203,22 +297,15 @@
             if k < outer_n - 2:
                 start_block(outer + 1 + k, c, k + 1, False, from_right)
 
-            if k == outer_n - 2:
-                for offset in range(1, INNER):
-                    print_copy(offset, c).wait_recv()
-
-                def multiply(i, total):
-                    for r in (c * piece + 2 * i, c * piece + 2 * i + 1):
-                        lanes = pl.ds(pl.multiple_of(r * TILE_LON, TILE_LON), TILE_LON)
-                        total = total + lax.dot_general(
-                            arr[:, lanes], tiles[r], (((1,), (1,)), ((), ())),
-                            preferred_element_type=jnp.float32,
-                        )
-                    return total
-
-                acc = lax.fori_loop(0, piece // 2, multiply, acc)
-
-    val[...] = jnp.dot(acc * sel[...], group[...], precision=lax.Precision.HIGHEST, preferred_element_type=jnp.float32)
+            if k >= outer_n - 3:
+                @pl.when(is_end if k == outer_n - 2 else jnp.logical_not(is_end))
+                def _():
+                    multiply(c)
+
+        if k == 0:
+            pl.when(is_next)(group_values)
+
+    val[...] = jnp.dot(acc[...] * sel[...], group[...], precision=lax.Precision.HIGHEST, preferred_element_type=jnp.float32)
 
     def value_copy(offset):
         to_rows = pl.ds(pl.multiple_of(lax.rem(inner + offset, INNER) * slots, slots), slots)
@@ -231,17 +318,30 @@
         value_copy(offset).wait_recv()
     out[...] = jnp.dot(weights[...], ret[...], precision=lax.Precision.HIGHEST, preferred_element_type=jnp.float32)
 
+    @pl.when(is_end)
+    def _():
+        for offset in range(INNER):
+            value_copy2(offset).wait_recv()
+        out[...] += jnp.dot(weights2[...], ret2[...], precision=lax.Precision.HIGHEST, preferred_element_type=jnp.float32)
+        for offset in range(INNER):
+            group_copy(offset).wait_send()
+
+    @pl.when(is_next)
+    def _():
+        for offset in range(INNER):
+            value_copy2(offset).wait_send()
+
     for offset in range(1, INNER):
         value_copy(offset).wait_send()
         for c in range(CHUNKS):
             print_copy(offset, c).wait_send()
     for k in range(outer_n - 1):
-        for c in range(CHUNKS):
-            @pl.when(jnp.logical_and(outer - k >= 0, has_right))
+        for c in range(PIECES):
+            @pl.when(goes(outer - k >= 0, k, True))
             def _():
                 block_copy(outer - k, c, k, True).wait_send()
 
-            @pl.when(jnp.logical_and(outer + k < outer_n, has_left))
+            @pl.when(goes(outer + k < outer_n, k, False))
             def _():
                 block_copy(outer + k, c, k, False).wait_send()
 
@@ -267,15 +367,36 @@
     src = lax.dynamic_slice_in_dim(tile_src.reshape(devices, slot_count), outer * INNER, INNER, 0)
     loc = lax.dynamic_slice_in_dim(tile_local.reshape(devices, slot_count), outer * INNER, INNER, 0)
     target = src % INNER
+    band_layer = src // INNER
+    beside = jnp.where(outer == 0, 1, jnp.where(outer == outer_n - 1, outer_n - 2, -1))
+    grouped = band_layer == beside
+    target = jnp.where(grouped, INNER + target, target)
     same = (target[:, :, None] == target[:, None, :]) & (order[None, :] < order[:, None])[None]
     rank = jnp.sum(same.astype(jnp.int32), axis=2)
     places = jnp.arange(slots, dtype=jnp.int32)
     my_target = lax.dynamic_index_in_dim(target, inner, 0, keepdims=False)
     my_rank = lax.dynamic_index_in_dim(rank, inner, 0, keepdims=False)
-    place = my_target * slots + my_rank
+    place = jnp.where(my_target < INNER, my_target * slots + my_rank, -1)
     hot = place[None, :] == jnp.arange(INNER * slots, dtype=jnp.int32)[:, None]
+    splits = GROUP_ROWS // cap
+    group_rows = jnp.arange(INNER * GROUP_ROWS, dtype=jnp.int32)
+    row_owner, row_split, row_slot = group_rows // GROUP_ROWS, group_rows % GROUP_ROWS // cap, group_rows % cap
+    in_group = (my_target[None, :] == INNER + row_owner[:, None]) & (my_rank[None, :] == row_slot[:, None])
+    hot2 = in_group[:, None, :] & (row_split[:, None] == jnp.arange(splits, dtype=jnp.int32)[None, :])[:, :, None]
+    hot2 = hot2.reshape(INNER * GROUP_ROWS, splits * slot_count)
+    from_layer = jnp.where(outer == 1, 0, outer_n - 1)
+    src_end = lax.dynamic_slice_in_dim(tile_src.reshape(devices, slot_count), from_layer * INNER, INNER, 0)
+    loc_end = lax.dynamic_slice_in_dim(tile_local.reshape(devices, slot_count), from_layer * INNER, INNER, 0)
+    to_me = src_end == me
+    rank_end = jnp.sum((to_me[:, None, :] & (order[None, :] < order[:, None])[None]).astype(jnp.int32), axis=2)
+    taken = to_me[:, None, :] & (rank_end[:, None, :] == jnp.arange(cap, dtype=jnp.int32)[None, :, None])
+    tile_end = jnp.sum(jnp.where(taken, loc_end[:, None, :] + 1, 0), axis=2) - 1
+    tile_end = jnp.broadcast_to(tile_end[:, None, :], (INNER, splits, cap)).reshape(INNER * GROUP_ROWS)
+    sel2 = (tile_end[None, :, None] == (jnp.arange(wide, dtype=jnp.int32) % LANES_T)[None, None, :]) & (
+        row_split[None, :, None] == jnp.arange(splits, dtype=jnp.int32)[:, None, None]
+    )
     chosen = (target[:, None, :] == inner) & (rank[:, None, :] == places[None, :, None])
-    code = (src // INNER) * LANES_T + loc + 1
+    code = band_layer * LANES_T + loc + 1
     named = jnp.sum(jnp.where(chosen, code[:, None, :], 0), axis=2).reshape(INNER * slots) - 1
     columns = jnp.arange(outer_n * wide, dtype=jnp.int32)
     column_code = (columns // wide) * LANES_T + columns % LANES_T
@@ -285,38 +406,47 @@
     mine = (order // KT)[None, :] == jnp.arange(stations, dtype=jnp.int32)[:, None]
     hits = (mine & live[None, :])[:, :, None] & (place[None, :, None] == jnp.arange(INNER * slots, dtype=jnp.int32)[None, None, :])
     weights = jnp.sum(hits.astype(jnp.float32), axis=1)
+    weights2 = jnp.sum(((mine & live[None, :])[:, None, :] & in_group[None]).astype(jnp.float32), axis=2)
 
     ext = rows + 2 * ITERS
     vmem = pl.BlockSpec(memory_space=pltpu.VMEM)
     dma = pltpu.SemaphoreType.DMA
     observed = pl.pallas_call(
-        functools.partial(kernel, outer_n, slots),
+        functools.partial(kernel, outer_n, slots, splits),
         out_shape=jax.ShapeDtypeStruct((stations, 128), jnp.float32),
-        in_specs=[pl.BlockSpec(memory_space=pltpu.SMEM)] + [vmem] * 7,
+        in_specs=[pl.BlockSpec(memory_space=pltpu.SMEM)] + [vmem] * 10,
         out_specs=vmem,
         scratch_shapes=[
             pltpu.VMEM((INNER * slots, footprint.shape[2]), jnp.bfloat16),
             pltpu.VMEM((INNER * slots, footprint.shape[2]), jnp.bfloat16),
+            pltpu.VMEM((INNER * GROUP_ROWS, footprint.shape[2] // splits), jnp.bfloat16),
+            pltpu.VMEM((INNER * GROUP_ROWS, footprint.shape[2] // splits), jnp.bfloat16),
             pltpu.VMEM((2, ITERS, wide, TILE_LON), jnp.bfloat16),
             pltpu.VMEM((2, ITERS, LANES_T, TILE_LON), jnp.float32),
             pltpu.VMEM((ext, wide, TILE_LON), jnp.float32),
             pltpu.VMEM((ext, wide, TILE_LON), jnp.float32),
             pltpu.VMEM((ext, LANES_T, TILE_LON), jnp.float32),
             pltpu.VMEM((rows, outer_n * wide, TILE_LON), jnp.bfloat16),
+            pltpu.VMEM((INNER * slots, outer_n * wide), jnp.float32),
             pltpu.VMEM((INNER * slots, 128), jnp.float32),
             pltpu.VMEM((INNER * slots, 128), jnp.float32),
+            pltpu.VMEM((INNER * GROUP_ROWS, 128), jnp.float32),
+            pltpu.VMEM((INNER * GROUP_ROWS, 128), jnp.float32),
             dma((INNER, CHUNKS)), dma((INNER, CHUNKS)),
+            dma((INNER,)), dma((INNER,)),
             dma((2, 2)), dma((2, 2)),
-            dma((outer_n - 1, CHUNKS)), dma((outer_n - 1, CHUNKS)),
-            dma((outer_n - 1, CHUNKS)), dma((outer_n - 1, CHUNKS)),
+            dma((outer_n - 1, PIECES)), dma((outer_n - 1, PIECES)),
+            dma((outer_n - 1, PIECES)), dma((outer_n - 1, PIECES)),
+            dma((INNER,)), dma((INNER,)),
             dma((INNER,)), dma((INNER,)),
         ],
         compiler_params=pltpu.CompilerParams(
-            collective_id=0, has_side_effects=True, vmem_limit_bytes=48 * 1024 * 1024
+            collective_id=0, has_side_effects=True, vmem_limit_bytes=50 * 1024 * 1024
         ),
     )(
         gates, footprint.reshape(slot_count, footprint.shape[2]), hot.astype(jnp.bfloat16),
-        flux_t, coef_t, sel, group.astype(jnp.float32), weights,
+        hot2.astype(jnp.bfloat16), flux_t, coef_t, sel, sel2.astype(jnp.float32), group.astype(jnp.float32),
+        weights, weights2,
     )
     return lax.all_gather(observed[:, :samples], "sample", axis=1, tiled=True)
 

time: 115 us -> 109 us (0.948)
  Pallas kernels: 103 us -> 94.5 us
    pallas_call x1, Pallas kernels: 103 us -> 94.5 us  [body(): pl.pallas_call(functools.partial(kernel, outer_n, slots, splits), out_sha...]
    reshape x1, local copies, waits for them, and re-layouts: 2.55 us -> 3.97 us  [body(): footprint.reshape(slot_count, footprint.shape[2])]
    unnamed x10 -> x6, local copies, waits for them, and re-layouts: 3.32 us -> 2.22 us
where the time goes in v3:
time: 109 us; the launch traced here: 108 us
  Pallas kernels  94.5 us (87%)
  local copies, waits for them, and re-layouts  11 us (10%)
  other arithmetic  2.63 us (2%)
    pallas_call x1, Pallas kernels, body(): pl.pallas_call(functools.partial(kernel, outer_n, slots, splits), out_sha...  94.5 us
    reshape x1, local copies, waits for them, and re-layouts, body(): footprint.reshape(slot_count, footprint.shape[2])  3.97 us
    unnamed x6, local copies, waits for them, and re-layouts  2.22 us

profile of v3, /device:TPU:0, one launch (start us, length us, event | category | flops | bytes accessed | tf_op | source)
XLA Modules:
  0.0 108.4 jit_solution(16403435619182675903)
XLA Ops:
  0.0 0.0 copy-start
  0.0 0.0 copy-start.1
  0.1 0.5 copy-done
  0.7 0.8 gather_fusion
  1.5 0.7 fusion.5.gates
  2.1 0.1 fusion.2.group
  2.2 0.8 copy.16
  3.1 0.1 reshape.542
  3.2 0.4 convert_reduce_fusion.2
  3.7 0.1 compare_and_fusion
  3.8 0.1 iota_compare_fusion.3
  3.9 0.2 convert_reduce_fusion.1.weights
  4.1 0.2 convert_reduce_fusion.weights2
  4.4 0.1 copy.20.hot2
  4.5 0.8 copy.18
  5.3 0.1 reshape.546
  5.5 0.2 select_reduce_fusion
  5.7 0.1 select_reduce_fusion.1
  5.9 0.1 sub.55
  6.0 0.1 copy.19
  6.1 0.1 eq.297
  6.2 0.1 broadcast_compare_fusion
  6.3 0.1 compare_convert_fusion.sel
  6.4 0.1 and_convert_fusion.sel2
  6.5 0.0 copy-done.1
  6.5 0.2 reshape.545
  6.8 2.2 %reshape.543 = bf16[4,32,7,512]{3,2,1,0:T(8,128)(2,1)S(1)} reshape(bf16[4,32,3584]{2,1,0:T(8,128)(2,1)} %param.7) | data formatting | bytes 1835008 | tf_op jit(solution)/shard_map/reshape | solution.py:361
  9.0 0.2 pad_bitcast_fusion.flux
  9.2 4.0 %reshape.541.prints = bf16[64,16384]{1,0:T(8,128)(2,1)} reshape(bf16[16,4,16384]{2,1,0:T(4,128)(2,1)} %param.10) | data formatting | bytes 4194304 | tf_op jit(solution)/shard_map/reshape | solution.py:447
  13.2 94.5 %shard_map.73 = f32[16,128]{1,0:T(8,128)S(1)} custom-call(f32[6,4]{1,0:T(8,128)S(1)} %fusion.5.gates, bf16[64,16384]{1,0:T(8,128)(2,1)} %reshape.541.prints, bf16[128,64]{1,0:T(8,128)(2,1)S(1)} %fusion.hot, bf16[128,256]{1,0:T(8,128)(2,1)S(1)} %copy.20.hot2, bf16[32,32,512]{2,1,0:T(8,128)(2,1)S(1)} %pad_bitcast_fusion.flux, f32[32,8,512]{2,1,0:T(8,128)S(1)} %pad.9.coef, ...), custom_call_target="tpu_custom_call" | custom-call | tf_op jit(solution)/shard_map/pallas_call | solution.py:414
  107.7 0.7 copy.21
  (22 shorter events, 0.2 us)
Async XLA Ops:
  0.0 0.7 copy-start
  0.0 6.5 %copy-start.1 = (f32[32,3584]{1,0:T(8,128)S(1)}, f32[32,3584]{1,0:T(8,128)}, u32[]{:S(2)}) copy-start(f32[32,3584]{1,0:T(8,128)} %param.8) | copy-start | bytes 1376260

commit v4 on v3

--- a/solution.py
+++ b/solution.py
@@ -13,7 +13,6 @@
 KT = 4
 ITERS = 6
 INNER = 8
-CHUNKS = 4
 PIECES = 8
 GROUP_ROWS = 16
 MESH = pl.DeviceIdType.MESH
@@ -36,7 +35,7 @@
 
 def kernel(
     outer_n, slots, splits,
-    gates, prints, hot, hot2, flux, coef, sel, sel2, group, weights, weights2,
+    steps, prints, hot, hot2, flux, coef, sel, sel2, group, weights, weights2,
     out,
     send, arr, send2, arr2, halo_f, halo_c, field_a, field_b, cof, tiles, acc, val, ret, val2, ret2,
     f_send, f_recv, g_send, g_recv, h_send, h_recv, r_send, r_recv, l_send, l_recv, v_send, v_recv, w_send, w_recv,
@@ -114,7 +113,13 @@
             halo_f[way] = jnp.zeros(halo_f.shape[1:], halo_f.dtype)
             halo_c[way] = jnp.zeros(halo_c.shape[1:], halo_c.dtype)
 
-    short = prints.shape[1] // splits
+    cells = prints.shape[2]
+    short = cells // splits
+
+    def some_prints(at):
+        block = prints[:, :, pl.ds(pl.multiple_of(at, 256), 256)]
+        return block.reshape(block.shape[0] * KT, 256)
+
     own2 = pl.ds(pl.multiple_of(inner * GROUP_ROWS, GROUP_ROWS), GROUP_ROWS)
 
     def rows2(offset):
@@ -128,7 +133,7 @@
         def pack2(i, carry):
             for j in range(2):
                 at = i * 512 + j * 256
-                stack = [prints[:, pl.ds(pl.multiple_of(q * short + at, 256), 256)] for q in range(splits)]
+                stack = [some_prints(q * short + at) for q in range(splits)]
                 packed = jnp.dot(hot2[...], jnp.concatenate(stack, axis=0), preferred_element_type=jnp.float32)
                 send2[:, pl.ds(pl.multiple_of(at, 256), 256)] = packed.astype(jnp.bfloat16)
             return carry
@@ -144,27 +149,24 @@
 
         lax.fori_loop(0, rows, clear, 0)
 
-    length = prints.shape[1] // CHUNKS
+    length = cells // PIECES
 
     def print_copy(offset, c):
         target = peer(offset)
-        lanes = pl.ds(c * length, length)
+        lanes = pl.ds(pl.multiple_of(c * length, length), length)
         to_rows = pl.ds(pl.multiple_of(lax.rem(inner + offset, INNER) * slots, slots), slots)
         my_rows = pl.ds(pl.multiple_of(inner * slots, slots), slots)
         return remote(send.at[to_rows, lanes], arr.at[my_rows, lanes], f_send.at[offset, c], f_recv.at[offset, c], target)
 
-    for c in range(CHUNKS):
-        def pack(i, carry):
-            for j in range(4):
-                lanes = pl.ds(pl.multiple_of(c * length + i * 1024 + j * 256, 256), 256)
-                send[:, lanes] = jnp.dot(hot[...], prints[:, lanes], preferred_element_type=jnp.float32).astype(jnp.bfloat16)
-            return carry
-
-        lax.fori_loop(0, length // 1024, pack, 0)
+    own = pl.ds(pl.multiple_of(inner * slots, slots), slots)
+
+    def send_prints(c):
+        for j in range(length // 256):
+            at = c * length + j * 256
+            packed = jnp.dot(hot[...], some_prints(at), preferred_element_type=jnp.float32)
+            send[:, pl.ds(pl.multiple_of(at, 256), 256)] = packed.astype(jnp.bfloat16)
         for offset in range(1, INNER):
             print_copy(offset, c).start()
-    own = pl.ds(pl.multiple_of(inner * slots, slots), slots)
-    arr[own, :] = send[own, :]
 
     def load(r, carry):
         field_a[r + ITERS] = flux[r].astype(jnp.float32)
@@ -197,18 +199,7 @@
         center = src[r, cut, :]
         west, east = east_west(center, lane, tile)
         lap = src[r - 1, cut, :] + src[r + 1, cut, :] + west + east - 4.0 * center
-        return center + gates[k, s] * cof[r] * lap
-
-    src, dst = field_a, field_b
-    for k in range(ITERS - 1):
-        def row_pair(i, carry, src=src, dst=dst, k=k):
-            for r in (k + 1 + 2 * i, k + 2 + 2 * i):
-                for s in range(samples):
-                    dst[r, s * LANES_T : (s + 1) * LANES_T, :] = updated(src, r, k, s)
-            return carry
-
-        lax.fori_loop(0, rows // 2 + ITERS - 1 - k, row_pair, 0)
-        src, dst = dst, src
+        return center + jnp.where(k < steps[s], 1.0, 0.0) * cof[r] * lap
 
     piece = rows // PIECES
 
@@ -230,21 +221,44 @@
             block_copy(block, c, k, to_right).start()
 
     mine = pl.ds(pl.multiple_of(outer * wide, wide), wide)
-    for c in range(PIECES):
-        def last_pair(i, carry, src=src):
-            for r in (c * piece + 2 * i, c * piece + 2 * i + 1):
-                done = [updated(src, r + ITERS, ITERS - 1, s) for s in range(samples)]
-                tiles[r, mine, :] = jnp.concatenate(done, axis=0).astype(jnp.bfloat16)
-            return carry
-
-        lax.fori_loop(0, piece // 2, last_pair, 0)
+
+    def step_row(r, k):
+        src, dst = (field_a, field_b) if k % 2 == 0 else (field_b, field_a)
+        done = [updated(src, r, k, s) for s in range(samples)]
+        if k == ITERS - 1:
+            tiles[r - ITERS, mine, :] = jnp.concatenate(done, axis=0).astype(jnp.bfloat16)
+        else:
+            for s in range(samples):
+                dst[r, s * LANES_T : (s + 1) * LANES_T, :] = done[s]
+
+    def send_piece(c):
         start_block(outer, c, 0, True, has_right)
         start_block(outer, c, 0, False, has_left)
 
+    for k in range(ITERS):
+        def row_pair(i, carry, k=k):
+            step_row(k + 1 + 2 * i, k)
+            step_row(k + 2 + 2 * i, k)
+            return carry
+
+        lax.fori_loop(0, piece // 2 + ITERS - 1 - k, row_pair, 0)
+    send_piece(0)
+    send_prints(0)
+
+    def next_piece(c, carry):
+        for k in range(ITERS):
+            for j in range(piece):
+                step_row(c * piece + 2 * ITERS - 1 - k + j, k)
+        send_piece(c)
+        send_prints(c)
+        return carry
+
+    lax.fori_loop(1, PIECES, next_piece, 0)
+    arr[own, :] = send[own, :]
+
     def multiply(c):
-        if c * CHUNKS % PIECES == 0:
-            for offset in range(1, INNER):
-                print_copy(offset, c * CHUNKS // PIECES).wait_recv()
+        for offset in range(1, INNER):
+            print_copy(offset, c).wait_recv()
         total = jnp.zeros(acc.shape, jnp.float32) if c == 0 else acc[...]
         for r in range(c * piece, (c + 1) * piece):
             total = total + lax.dot_general(
@@ -333,7 +347,7 @@
 
     for offset in range(1, INNER):
         value_copy(offset).wait_send()
-        for c in range(CHUNKS):
+        for c in range(PIECES):
             print_copy(offset, c).wait_send()
     for k in range(outer_n - 1):
         for c in range(PIECES):
@@ -361,11 +375,11 @@
     flux_t = flux.reshape(samples, rows, TILES_DEV, TILE_LON).transpose(1, 0, 2, 3)
     flux_t = jnp.pad(flux_t, ((0, 0), (0, 0), (0, 1), (0, 0))).reshape(rows, wide, TILE_LON)
     coef_t = jnp.pad(coeff.reshape(rows, TILES_DEV, TILE_LON), ((0, 0), (0, 1), (0, 0)))
-    gates = (jnp.arange(ITERS, dtype=jnp.int32)[:, None] < diff_steps[None, :]).astype(jnp.float32)
 
     order = jnp.arange(slot_count, dtype=jnp.int32)
-    src = lax.dynamic_slice_in_dim(tile_src.reshape(devices, slot_count), outer * INNER, INNER, 0)
-    loc = lax.dynamic_slice_in_dim(tile_local.reshape(devices, slot_count), outer * INNER, INNER, 0)
+    listed = (tile_src[:, :, 0] * LANES_T + tile_local).reshape(devices, slot_count)
+    here = lax.dynamic_slice_in_dim(listed, outer * INNER, INNER, 0)
+    src, loc = here // LANES_T, here % LANES_T
     target = src % INNER
     band_layer = src // INNER
     beside = jnp.where(outer == 0, 1, jnp.where(outer == outer_n - 1, outer_n - 2, -1))
@@ -385,8 +399,8 @@
     hot2 = in_group[:, None, :] & (row_split[:, None] == jnp.arange(splits, dtype=jnp.int32)[None, :])[:, :, None]
     hot2 = hot2.reshape(INNER * GROUP_ROWS, splits * slot_count)
     from_layer = jnp.where(outer == 1, 0, outer_n - 1)
-    src_end = lax.dynamic_slice_in_dim(tile_src.reshape(devices, slot_count), from_layer * INNER, INNER, 0)
-    loc_end = lax.dynamic_slice_in_dim(tile_local.reshape(devices, slot_count), from_layer * INNER, INNER, 0)
+    there = lax.dynamic_slice_in_dim(listed, from_layer * INNER, INNER, 0)
+    src_end, loc_end = there // LANES_T, there % LANES_T
     to_me = src_end == me
     rank_end = jnp.sum((to_me[:, None, :] & (order[None, :] < order[:, None])[None]).astype(jnp.int32), axis=2)
     taken = to_me[:, None, :] & (rank_end[:, None, :] == jnp.arange(cap, dtype=jnp.int32)[None, :, None])
@@ -402,7 +416,7 @@
     column_code = (columns // wide) * LANES_T + columns % LANES_T
     sel = (named[:, None] == column_code[None, :]).astype(jnp.float32)
     group = ((columns % wide) // LANES_T)[:, None] == jnp.arange(128, dtype=jnp.int32)[None, :]
-    live = order % KT < tile_count[order // KT]
+    live = (jnp.arange(KT, dtype=jnp.int32)[None, :] < tile_count[:, None]).reshape(slot_count)
     mine = (order // KT)[None, :] == jnp.arange(stations, dtype=jnp.int32)[:, None]
     hits = (mine & live[None, :])[:, :, None] & (place[None, :, None] == jnp.arange(INNER * slots, dtype=jnp.int32)[None, None, :])
     weights = jnp.sum(hits.astype(jnp.float32), axis=1)
@@ -432,7 +446,7 @@
             pltpu.VMEM((INNER * slots, 128), jnp.float32),
             pltpu.VMEM((INNER * GROUP_ROWS, 128), jnp.float32),
             pltpu.VMEM((INNER * GROUP_ROWS, 128), jnp.float32),
-            dma((INNER, CHUNKS)), dma((INNER, CHUNKS)),
+            dma((INNER, PIECES)), dma((INNER, PIECES)),
             dma((INNER,)), dma((INNER,)),
             dma((2, 2)), dma((2, 2)),
             dma((outer_n - 1, PIECES)), dma((outer_n - 1, PIECES)),
@@ -444,7 +458,7 @@
             collective_id=0, has_side_effects=True, vmem_limit_bytes=50 * 1024 * 1024
         ),
     )(
-        gates, footprint.reshape(slot_count, footprint.shape[2]), hot.astype(jnp.bfloat16),
+        diff_steps, footprint, hot.astype(jnp.bfloat16),
         hot2.astype(jnp.bfloat16), flux_t, coef_t, sel, sel2.astype(jnp.float32), group.astype(jnp.float32),
         weights, weights2,
     )

time: 109 us -> 99.4 us (0.912)
  local copies, waits for them, and re-layouts: 11 us -> 4.15 us
  Pallas kernels: 94.5 us -> 91.9 us
    reshape x3 -> x1, local copies, waits for them, and re-layouts: 4.27 us -> 0.15 us  [body(): (tile_src[:, :, 0] * LANES_T + tile_local).reshape(devices, slot_count)]
    pallas_call x1, Pallas kernels: 94.5 us -> 91.9 us  [body(): pl.pallas_call(functools.partial(kernel, outer_n, slots, splits), out_sha...]
    unnamed x6, local copies, waits for them, and re-layouts: 2.22 us -> 0.02 us
where the time goes in v4:
time: 99.4 us; the launch traced here: 99.2 us
  Pallas kernels  91.9 us (92%)
  local copies, waits for them, and re-layouts  4.15 us (4%)
  other arithmetic  2.77 us (3%)
    pallas_call x1, Pallas kernels, body(): pl.pallas_call(functools.partial(kernel, outer_n, slots, splits), out_sha...  91.9 us
    reshape x1, local copies, waits for them, and re-layouts, body(): flux.reshape(samples, rows, TILES_DEV, TILE_LON).transpose(1, 0, 2, 3)  2.19 us

profile of v4, /device:TPU:0, one launch (start us, length us, event | category | flops | bytes accessed | tf_op | source)
XLA Modules:
  0.0 99.2 jit_solution(5634361215532773289)
XLA Ops:
  0.0 0.7 bitcast_add_fusion
  0.7 0.1 copy.18
  0.9 0.2 reshape.494
  1.2 0.4 convert_reduce_fusion.2
  1.7 0.1 compare_and_fusion
  1.8 0.0 copy-start.1
  1.8 0.1 copy.21.hot2
  2.0 2.2 %reshape.495 = bf16[4,32,7,512]{3,2,1,0:T(8,128)(2,1)S(1)} reshape(bf16[4,32,3584]{2,1,0:T(8,128)(2,1)} %param.7) | data formatting | bytes 1835008 | tf_op jit(solution)/shard_map/reshape | solution.py:375
  4.1 0.0 copy-start.2
  4.2 0.0 copy-start
  4.2 0.2 pad_bitcast_fusion.flux
  4.4 0.0 copy-done.1
  4.4 0.2 reshape.497
  4.7 0.2 select_reduce_fusion
  4.9 0.1 sub.60
  5.0 0.1 compare_convert_fusion.sel
  5.1 0.1 select_reduce_fusion.1
  5.3 0.1 copy.20
  5.4 0.1 eq.297
  5.5 0.1 broadcast_compare_fusion
  5.6 0.1 and_convert_fusion.sel2
  5.7 0.1 fusion.2.group
  5.8 0.1 iota_compare_fusion.3
  5.9 0.0 copy-done.2
  5.9 0.1 iota_compare_fusion.6
  6.0 0.1 lt.142
  6.1 0.2 convert_reduce_fusion.1.weights
  6.3 0.2 convert_reduce_fusion.weights2
  6.6 0.0 copy-done
  6.6 91.9 %shard_map.73 = f32[16,128]{1,0:T(8,128)S(1)} custom-call(s32[4]{0:T(128)S(1)} %copy-done, bf16[16,4,16384]{2,1,0:T(4,128)(2,1)} %prints.1, bf16[128,64]{1,0:T(8,128)(2,1)S(1)} %fusion.hot, bf16[128,256]{1,0:T(8,128)(2,1)S(1)} %copy.21.hot2, bf16[32,32,512]{2,1,0:T(8,128)(2,1)S(1)} %pad_bitcast_fusion.flux, f32[32,8,512]{2,1,0:T(8,128)S(1)} %pad.9.coef, ...), custom_call_target="tpu_custom_call" | custom-call | tf_op jit(solution)/shard_map/pallas_call | solution.py:428
  98.5 0.7 copy.22
  (20 shorter events, 0.3 us)
Async XLA Ops:
  1.8 2.6 %copy-start.1 = (f32[32,3584]{1,0:T(8,128)S(1)}, f32[32,3584]{1,0:T(8,128)}, u32[]{:S(2)}) copy-start(f32[32,3584]{1,0:T(8,128)} %param.8) | copy-start | bytes 1376260
  4.1 1.8 %copy-start.2 = (s32[16]{0:T(128)S(1)}, s32[16]{0:T(128)}, u32[]{:S(2)}) copy-start(s32[16]{0:T(128)} %param.13) | copy-start | bytes 196
  4.2 2.4 %copy-start = (s32[4]{0:T(128)S(1)}, s32[4]{0:T(128)}, u32[]{:S(2)}) copy-start(s32[4]{0:T(128)} %steps.1) | copy-start | bytes 52
